TPU v7x, 32 devices: a whole 2x2x4 slice. The times are simulated.
32 devices in a mesh: segment: 2 (over x), space: 8 (over z, core), mirror: 2 (over y).
Axes of the slice: x: 2, y: 2, z: 4, core: 2. Of those that a mesh axis runs over, the one named last changes fastest.
Arguments:
- arrivals: bfloat16 [2, 2, 128, 128, 256], P('mirror', 'segment', 'space'), may hold values from -6 to 6
- stashed: bfloat16 [2, 2, 128, 128, 256], P('mirror', 'segment', 'space'), may hold values from -6 to 6
- weights: bfloat16 [2, 2, 2, 3, 3, 256, 256], P('mirror', 'segment'), may hold values from -0.125 to 0.125
Outputs:
- departures: bfloat16 [2, 2, 128, 128, 256], P('mirror', 'segment', 'space')
- grad_sum: float32 [2, 2, 256, 2, 3, 3, 256], P('mirror', 'segment', 'space')
All inputs are finite; a program needn't handle non-finite values.
Results may differ from a plain program's by a relative error of at most 0.0053.
Values may be sent and summed in bfloat16 or wider, within the bound.
A program may use at most 128 MiB of HBM per device.

v0:
```python
import functools
import math

import jax
import jax.numpy as jnp
from jax import lax
from jax.experimental import pallas as pl
from jax.experimental.pallas import tpu as pltpu
from jax.sharding import PartitionSpec as P

F32 = jnp.float32
BF16 = jnp.bfloat16
MESH = pl.DeviceIdType.MESH


def divisor(total, most):
    return max(d for d in range(1, most + 1) if total % d == 0)


def kernel(
    sizes,
    arr,
    sta,
    wts,
    out,
    gout,
    a_buf,
    s_buf,
    r_buf,
    w3,
    wt3,
    x3,
    y3,
    slope,
    x_t,
    h_t,
    send_buf,
    gacc,
    gsend,
    pair_in,
    zsend,
    zrecv,
    owned,
    psend,
    precv,
    load_sem,
    halo_s,
    halo_r,
    swap_s,
    swap_r,
    pair_s,
    pair_r,
    z_s,
    z_r,
    part_s,
    part_r,
):
    rows, cols, ch, n, scale = sizes
    nz, share = n // 2, ch // n
    me = lax.axis_index("space")
    seg = lax.axis_index("segment")
    mir = lax.axis_index("mirror")
    parity, mine = lax.rem(me, 2), lax.div(me, 2)
    lead = seg == mir
    has_up, has_down = me > 0, me < n - 1
    out_rows = divisor(rows, 4)
    chunks = rows // out_rows
    pre_rows = divisor(rows + 2, 6)
    partner = {"segment": 1 - seg}
    twin = {"segment": 1 - seg, "mirror": 1 - mir}

    def span(first, count):
        return pl.ds(pl.multiple_of(first * cols, cols), count * cols)

    loads = [
        pltpu.make_async_copy(arr, a_buf.at[span(2, rows)], load_sem.at[0]),
        pltpu.make_async_copy(sta, s_buf.at[span(2, rows)], load_sem.at[1]),
        pltpu.make_async_copy(wts, w3, load_sem.at[2]),
    ]
    for load in loads:
        load.start()

    barrier = pltpu.get_barrier_semaphore()
    for k in range(1, n):
        pl.semaphore_signal(
            barrier, inc=1, device_id={"space": lax.rem(me + k, n)}, device_id_type=MESH
        )
    pl.semaphore_signal(barrier, inc=1, device_id=partner, device_id_type=MESH)
    pl.semaphore_signal(barrier, inc=1, device_id=twin, device_id_type=MESH)
    pl.semaphore_wait(barrier, n + 1)

    def up_copy(i, src, first, buf):
        return pltpu.make_async_remote_copy(
            src_ref=src.at[span(first, 2)],
            dst_ref=buf.at[span(rows + 2, 2)],
            send_sem=halo_s.at[i, 0],
            recv_sem=halo_r.at[i, 0],
            device_id={"space": me - 1},
            device_id_type=MESH,
        )

    def down_copy(i, src, first, buf):
        return pltpu.make_async_remote_copy(
            src_ref=src.at[span(first + rows - 2, 2)],
            dst_ref=buf.at[span(0, 2)],
            send_sem=halo_s.at[i, 1],
            recv_sem=halo_r.at[i, 1],
            device_id={"space": me + 1},
            device_id_type=MESH,
        )

    def halo_send_up(i, src, first, buf):
        @pl.when(has_up)
        def _():
            up_copy(i, src, first, buf).start()

    def halo_send_down(i, src, first, buf):
        @pl.when(has_down)
        def _():
            down_copy(i, src, first, buf).start()

    def halo_wait(i, src, first, buf):
        @pl.when(has_down)
        def _():
            up_copy(i, src, first, buf).wait_recv()

        @pl.when(has_up)
        def _():
            down_copy(i, src, first, buf).wait_recv()

        zeros = jnp.zeros((2 * cols, ch), BF16)

        @pl.when(jnp.logical_not(has_up))
        def _():
            buf[span(0, 2), :] = zeros

        @pl.when(jnp.logical_not(has_down))
        def _():
            buf[span(rows + 2, 2), :] = zeros

    def halo_drain(i, src, first, buf):
        @pl.when(has_up)
        def _():
            up_copy(i, src, first, buf).wait_send()

        @pl.when(has_down)
        def _():
            down_copy(i, src, first, buf).wait_send()

    halo_send_up(0, arr, 0, a_buf)
    halo_send_down(0, arr, 0, a_buf)
    halo_send_up(1, sta, 0, s_buf)
    halo_send_down(1, sta, 0, s_buf)

    loads[2].wait()

    @pl.loop(0, 2)
    def _(j):
        for a in range(3):
            for b in range(3):
                tile = w3[j, 2 - a, (2 - b) * ch : (3 - b) * ch, :]
                wt3[j, a, b * ch : (b + 1) * ch, :] = tile.T

    loads[0].wait()
    loads[1].wait()
    halo_wait(0, arr, 0, a_buf)
    halo_wait(1, sta, 0, s_buf)

    def widen(val, dst, first, count):
        shape = (count, cols, ch)
        col = lax.broadcasted_iota(jnp.int32, shape, 1)
        left = pltpu.roll(val, 1, 0).reshape(shape)
        right = pltpu.roll(val, count * cols - 1, 0).reshape(shape)
        flat = (count * cols, ch)
        dst[span(first, count), 0:ch] = (
            jnp.where(col == 0, 0.0, left).astype(BF16).reshape(flat)
        )
        dst[span(first, count), ch : 2 * ch] = val.astype(BF16)
        dst[span(first, count), 2 * ch : 3 * ch] = (
            jnp.where(col == cols - 1, 0.0, right).astype(BF16).reshape(flat)
        )

    def widen_all(src, dst):
        step = divisor(rows + 4, 4)

        @pl.loop(0, (rows + 4) // step)
        def _(k):
            widen(src[span(k * step, step), :].astype(F32), dst, k * step, step)

    def conv(src, kern, j, first, count):
        total = None
        for a in range(3):
            term = jnp.dot(
                src[span(first + a, count), :], kern[j, a], preferred_element_type=F32
            )
            total = term if total is None else total + term
        return total

    def clear_outside(dst):
        zeros = jnp.zeros((cols, 3 * ch), BF16)

        @pl.when(jnp.logical_not(has_up))
        def _():
            dst[span(0, 1), :] = zeros

        @pl.when(jnp.logical_not(has_down))
        def _():
            dst[span(rows + 1, 1), :] = zeros

    def transposed(dst, src, first, lanes):
        @pl.loop(0, chunks)
        def _(k):
            block = src[span(first + k * out_rows, out_rows), lanes]
            dst[:, span(k * out_rows, out_rows)] = block.T

    def hidden_forward(src3, dst3):
        @pl.loop(0, (rows + 2) // pre_rows)
        def _(k):
            pre = conv(src3, w3, 0, k * pre_rows, pre_rows)
            widen(pre * jax.nn.sigmoid(pre), dst3, k * pre_rows, pre_rows)

        clear_outside(dst3)

    def hidden_backward(src3, dst):
        @pl.loop(0, (rows + 2) // pre_rows)
        def _(k):
            pre = conv(src3, w3, 0, k * pre_rows, pre_rows)
            sig = jax.nn.sigmoid(pre)
            slope[span(k * pre_rows, pre_rows), :] = sig * (1.0 + pre * (1.0 - sig))
            dst[span(k * pre_rows, pre_rows), 0:ch] = (pre * sig).astype(BF16)

    def inner_backward(g3, dst3):
        @pl.loop(0, (rows + 2) // pre_rows)
        def _(k):
            val = conv(g3, wt3, 1, k * pre_rows, pre_rows)
            widen(val * slope[span(k * pre_rows, pre_rows), :], dst3, k * pre_rows, pre_rows)

        clear_outside(dst3)

    def swap_copy(k):
        return pltpu.make_async_remote_copy(
            src_ref=send_buf.at[span(k * out_rows, out_rows)],
            dst_ref=r_buf.at[span(2 + k * out_rows, out_rows)],
            send_sem=swap_s.at[k],
            recv_sem=swap_r.at[k],
            device_id=partner,
            device_id_type=MESH,
        )

    def finish_section(base, src3, kern, j, sending):
        @pl.loop(0, chunks)
        def _(step):
            k = lax.rem(chunks - step, chunks)
            val = base[span(2 + k * out_rows, out_rows), :].astype(F32)
            val = (val + conv(src3, kern, j, k * out_rows, out_rows)).astype(BF16)
            if sending:
                send_buf[span(k * out_rows, out_rows), :] = val
                swap_copy(k).start()
            else:
                out[span(k * out_rows, out_rows), :] = val

    def receive():
        swap_copy(0).wait_recv()
        if chunks > 1:
            swap_copy(chunks - 1).wait_recv()
        halo_send_up(2, r_buf, 2, r_buf)
        halo_send_down(2, r_buf, 2, r_buf)
        for k in range(1, chunks - 1):
            swap_copy(k).wait_recv()
        halo_wait(2, r_buf, 2, r_buf)

    def weight_grad(j, lhs_t, src3, first):
        @pl.loop(0, 3)
        def _(a):
            for b in range(3):
                val = scale * jnp.dot(
                    lhs_t[...],
                    src3[span(first + a, rows), b * ch : (b + 1) * ch],
                    preferred_element_type=F32,
                )
                lanes = pl.ds(pl.multiple_of(((2 - a) * 3 + (2 - b)) * ch, ch), ch)
                for owner in range(n):
                    gacc[j, owner % 2, owner // 2, :, lanes] = val[
                        owner * share : (owner + 1) * share
                    ]

    def pair_copy(j):
        return pltpu.make_async_remote_copy(
            src_ref=gsend.at[j],
            dst_ref=pair_in.at[j],
            send_sem=pair_s.at[j],
            recv_sem=pair_r.at[j],
            device_id={"space": me + 1 - 2 * parity},
            device_id_type=MESH,
        )

    def z_copy(j, k):
        return pltpu.make_async_remote_copy(
            src_ref=zsend.at[j, k],
            dst_ref=zrecv.at[j, k],
            send_sem=z_s.at[j, k],
            recv_sem=z_r.at[j, k],
            device_id={"space": 2 * lax.rem(mine + k + 1, nz) + parity},
            device_id_type=MESH,
        )

    def part_copy(j):
        return pltpu.make_async_remote_copy(
            src_ref=psend.at[j],
            dst_ref=precv.at[j],
            send_sem=part_s.at[j],
            recv_sem=part_r.at[j],
            device_id=twin,
            device_id_type=MESH,
        )

    def grads_to_pair(j):
        @pl.loop(0, nz)
        def _(z):
            gsend[j, z] = gacc[j, 1 - parity, z].astype(BF16)

        pair_copy(j).start()

    def grads_to_line(j):
        pair_copy(j).wait_recv()

        @pl.loop(0, nz - 1)
        def _(k):
            z = lax.rem(mine + k + 1, nz)
            zsend[j, k] = (gacc[j, parity, z] + pair_in[j, z].astype(F32)).astype(BF16)
            z_copy(j, k).start()

        owned[j] = gacc[j, parity, mine] + pair_in[j, mine].astype(F32)

    def grads_to_twin(j):
        total = owned[j]
        for k in range(nz - 1):
            z_copy(j, k).wait_recv()
            total = total + zrecv[j, k].astype(F32)
        owned[j] = total
        psend[j] = total.astype(BF16)
        part_copy(j).start()

    def grads_finish(j):
        part_copy(j).wait_recv()
        gout[j] = owned[j] + precv[j].astype(F32)

    mid = slice(0, ch)

    @pl.when(lead)
    def _():
        widen_all(a_buf, x3)
        hidden_forward(x3, y3)
        finish_section(a_buf, y3, w3, 1, True)
        widen_all(s_buf, x3)
        hidden_backward(x3, y3)
        transposed(h_t, y3, 1, mid)
        transposed(x_t, s_buf, 2, mid)
        receive()
        widen_all(r_buf, x3)
        weight_grad(1, h_t, x3, 1)
        grads_to_pair(1)
        inner_backward(x3, y3)
        grads_to_line(1)
        weight_grad(0, x_t, y3, 0)
        grads_to_pair(0)
        finish_section(r_buf, y3, wt3, 0, False)
        grads_to_line(0)

    @pl.when(jnp.logical_not(lead))
    def _():
        widen_all(s_buf, x3)
        hidden_backward(x3, y3)
        transposed(h_t, y3, 1, mid)
        widen_all(a_buf, x3)
        inner_backward(x3, y3)
        finish_section(a_buf, y3, wt3, 0, True)
        weight_grad(1, h_t, x3, 1)
        grads_to_pair(1)
        transposed(x_t, s_buf, 2, mid)
        weight_grad(0, x_t, y3, 0)
        grads_to_line(1)
        grads_to_pair(0)
        grads_to_line(0)
        receive()
        widen_all(r_buf, x3)
        hidden_forward(x3, y3)
        finish_section(r_buf, y3, w3, 1, False)

    grads_to_twin(1)
    grads_to_twin(0)
    grads_finish(1)
    grads_finish(0)

    halo_drain(0, arr, 0, a_buf)
    halo_drain(1, sta, 0, s_buf)
    halo_drain(2, r_buf, 2, r_buf)
    for k in range(chunks):
        swap_copy(k).wait_send()
    for j in range(2):
        pair_copy(j).wait_send()
        part_copy(j).wait_send()
        for k in range(nz - 1):
            z_copy(j, k).wait_send()


def body(arrivals, stashed, weights):
    _, _, rows, cols, ch = arrivals.shape
    n = lax.axis_size("space")
    nz, share = n // 2, ch // n
    scale = 1.0 / math.sqrt(rows * n * cols)
    out_chunks = rows // divisor(rows, 4)
    cells = rows * cols
    wide = 9 * ch
    dma = pltpu.SemaphoreType.DMA
    vm = pltpu.VMEM
    halo_cells = (rows + 4) * cols
    out, grads = pl.pallas_call(
        functools.partial(kernel, (rows, cols, ch, n, scale)),
        out_shape=(
            jax.ShapeDtypeStruct((cells, ch), BF16),
            jax.ShapeDtypeStruct((2, share, wide), F32),
        ),
        in_specs=[pl.BlockSpec(memory_space=pl.ANY)] * 3,
        out_specs=(pl.BlockSpec(memory_space=pltpu.VMEM),) * 2,
        scratch_shapes=[
            vm((halo_cells, ch), BF16),
            vm((halo_cells, ch), BF16),
            vm((halo_cells, ch), BF16),
            vm((2, 3, 3 * ch, ch), BF16),
            vm((2, 3, 3 * ch, ch), BF16),
            vm((halo_cells, 3 * ch), BF16),
            vm((halo_cells, 3 * ch), BF16),
            vm(((rows + 2) * cols, ch), F32),
            vm((ch, cells), BF16),
            vm((ch, cells), BF16),
            vm((cells, ch), BF16),
            vm((2, 2, nz, share, wide), F32),
            vm((2, nz, share, wide), BF16),
            vm((2, nz, share, wide), BF16),
            vm((2, nz - 1, share, wide), BF16),
            vm((2, nz - 1, share, wide), BF16),
            vm((2, share, wide), F32),
            vm((2, share, wide), BF16),
            vm((2, share, wide), BF16),
            dma((3,)),
            dma((3, 2)),
            dma((3, 2)),
            dma((out_chunks,)),
            dma((out_chunks,)),
            dma((2,)),
            dma((2,)),
            dma((2, nz - 1)),
            dma((2, nz - 1)),
            dma((2,)),
            dma((2,)),
        ],
        compiler_params=pltpu.CompilerParams(
            collective_id=0, has_side_effects=True, vmem_limit_bytes=56 * 1024 * 1024
        ),
    )(
        arrivals.reshape(cells, ch),
        stashed.reshape(cells, ch),
        weights.reshape(2, 3, 3 * ch, ch),
    )
    grads = jnp.transpose(grads.reshape(2, share, 3, 3, ch), (1, 0, 2, 3, 4))
    return (out.reshape(arrivals.shape), grads[None, None])


def solution(mesh):
    in_specs = (
        P("mirror", "segment", "space", None, None),
        P("mirror", "segment", "space", None, None),
        P("mirror", "segment", None, None, None, None, None),
    )
    out_specs = (
        P("mirror", "segment", "space", None, None),
        P("mirror", "segment", "space", None, None, None, None),
    )
    return jax.shard_map(body, mesh=mesh, in_specs=in_specs, out_specs=out_specs, check_vma=False)
```

profile of v0, /device:TPU:24, one launch (start us, length us, event | category | flops | bytes accessed | tf_op | source)
XLA Modules:
  0.0 85.3 jit_solution(13464313300757037109)
XLA Ops:
  0.6 80.9 %shard_map.50 = (bf16[2048,256]{1,0:T(8,128)(2,1)}, f32[2,32,2304]{2,1,0:T(8,128)}) custom-call(bf16[2048,256]{1,0:T(8,128)(2,1)} %bitcast.9, bf16[2048,256]{1,0:T(8,128)(2,1)} %bitcast.10, bf16[2,3,768,256]{3,2,1,0:T(8,128)(2,1)} %bitcast.8), custom_call_target="tpu_custom_call" | custom-call | tf_op jit(solution)/shard_map/pallas_call | solution.py:418
  81.6 0.0 copy-start
  81.6 1.5 %reshape.23 = f32[2,32,3,3,256]{4,3,2,1,0:T(4,128)S(1)} reshape(f32[2,32,2304]{2,1,0:T(8,128)} %get-tuple-element.5) | data formatting | bytes 1179648 | tf_op jit(solution)/shard_map/reshape | solution.py:466
  83.0 1.3 %copy.6 = f32[1,1,32,2,3,3,256]{6,3,5,4,2,1,0:T(2,128)} copy(f32[1,1,32,2,3,3,256]{6,5,4,2,3,1,0:T(4,128)S(1)} %bitcast.7) | data formatting | bytes 1179648
  84.3 0.0 copy-done
  84.3 1.0 %copy.8 = bf16[1,1,16,128,256]{4,3,2,1,0:T(8,128)(2,1)} copy(bf16[1,1,16,128,256]{4,3,2,1,0:T(8,128)(2,1)S(1)} %bitcast.11) | data formatting | bytes 2097152
Async XLA Ops:
  81.6 2.7 %copy-start = (bf16[2048,256]{1,0:T(8,128)(2,1)S(1)}, bf16[2048,256]{1,0:T(8,128)(2,1)}, u32[]{:S(2)}) copy-start(bf16[2048,256]{1,0:T(8,128)(2,1)} %get-tuple-element.4) | copy-start | bytes 3145732
where the time goes:
time: 85.4 us; the launch traced here: 85.3 us
  Pallas kernels  80.9 us (95%)
  local copies, waits for them, and re-layouts  3.7 us (4%)
    pallas_call x1, Pallas kernels, body(): pl.pallas_call(functools.partial(kernel, (rows, cols, ch, n, scale)), out...  80.9 us
    unnamed x4, local copies, waits for them, and re-layouts  2.25 us

commit v1 on v0

--- a/solution.py
+++ b/solution.py
@@ -32,6 +32,7 @@
     x3,
     y3,
     slope,
+    h_buf,
     x_t,
     h_t,
     send_buf,
@@ -41,8 +42,11 @@
     zsend,
     zrecv,
     owned,
+    tsend,
+    trecv,
     psend,
     precv,
+    relay_in,
     load_sem,
     halo_s,
     halo_r,
@@ -54,6 +58,12 @@
     z_r,
     part_s,
     part_r,
+    diag_s,
+    diag_r,
+    relay_s,
+    relay_r,
+    onward_s,
+    onward_r,
 ):
     rows, cols, ch, n, scale = sizes
     nz, share = n // 2, ch // n
@@ -65,9 +75,14 @@
     has_up, has_down = me > 0, me < n - 1
     out_rows = divisor(rows, 4)
     chunks = rows // out_rows
+    piece = out_rows // 2
+    half = 9 * ch // 2
+    my_lanes = pl.ds(pl.multiple_of(mir * half, half), half)
+    twin_lanes = pl.ds(pl.multiple_of((1 - mir) * half, half), half)
     pre_rows = divisor(rows + 2, 6)
     partner = {"segment": 1 - seg}
     twin = {"segment": 1 - seg, "mirror": 1 - mir}
+    relay = {"mirror": 1 - mir}
 
     def span(first, count):
         return pl.ds(pl.multiple_of(first * cols, cols), count * cols)
@@ -87,7 +102,8 @@
         )
     pl.semaphore_signal(barrier, inc=1, device_id=partner, device_id_type=MESH)
     pl.semaphore_signal(barrier, inc=1, device_id=twin, device_id_type=MESH)
-    pl.semaphore_wait(barrier, n + 1)
+    pl.semaphore_signal(barrier, inc=1, device_id=relay, device_id_type=MESH)
+    pl.semaphore_wait(barrier, n + 2)
 
     def up_copy(i, src, first, buf):
         return pltpu.make_async_remote_copy(
@@ -154,12 +170,17 @@
 
     loads[2].wait()
 
-    @pl.loop(0, 2)
-    def _(j):
-        for a in range(3):
-            for b in range(3):
-                tile = w3[j, 2 - a, (2 - b) * ch : (3 - b) * ch, :]
-                wt3[j, a, b * ch : (b + 1) * ch, :] = tile.T
+    def transpose_kernels():
+        @pl.loop(0, 2)
+        def _(j):
+            for a in range(3):
+                for b in range(3):
+                    tile = w3[j, 2 - a, (2 - b) * ch : (3 - b) * ch, :]
+                    wt3[j, a, b * ch : (b + 1) * ch, :] = tile.T
+
+    @pl.when(jnp.logical_not(lead))
+    def _():
+        transpose_kernels()
 
     loads[0].wait()
     loads[1].wait()
@@ -237,36 +258,89 @@
 
         clear_outside(dst3)
 
-    def swap_copy(k):
-        return pltpu.make_async_remote_copy(
-            src_ref=send_buf.at[span(k * out_rows, out_rows)],
-            dst_ref=r_buf.at[span(2 + k * out_rows, out_rows)],
-            send_sem=swap_s.at[k],
-            recv_sem=swap_r.at[k],
+    def swap_copy(q):
+        return pltpu.make_async_remote_copy(
+            src_ref=send_buf.at[span(q * piece, piece)],
+            dst_ref=r_buf.at[span(2 + q * piece, piece)],
+            send_sem=swap_s.at[q],
+            recv_sem=swap_r.at[q],
             device_id=partner,
             device_id_type=MESH,
         )
 
-    def finish_section(base, src3, kern, j, sending):
+    def relay_copy(k):
+        return pltpu.make_async_remote_copy(
+            src_ref=send_buf.at[span((2 * k + 1) * piece, piece)],
+            dst_ref=relay_in.at[k],
+            send_sem=relay_s.at[k],
+            recv_sem=relay_r.at[k],
+            device_id=relay,
+            device_id_type=MESH,
+        )
+
+    def onward_copy(k):
+        return pltpu.make_async_remote_copy(
+            src_ref=relay_in.at[k],
+            dst_ref=r_buf.at[span(2 + (2 * k + 1) * piece, piece)],
+            send_sem=onward_s.at[k],
+            recv_sem=onward_r.at[k],
+            device_id=twin,
+            device_id_type=MESH,
+        )
+
+    relayed = [0] + list(range(chunks - 2, 0, -1))
+    direct_late = [q for q in range(2, 2 * chunks - 2)]
+    direct_back = [q for q in range(2 * chunks) if q % 2 == 0 or q == 2 * chunks - 1]
+
+    def finish_section(base, src3, kern, j, role):
         @pl.loop(0, chunks)
         def _(step):
             k = lax.rem(chunks - step, chunks)
             val = base[span(2 + k * out_rows, out_rows), :].astype(F32)
             val = (val + conv(src3, kern, j, k * out_rows, out_rows)).astype(BF16)
-            if sending:
-                send_buf[span(k * out_rows, out_rows), :] = val
-                swap_copy(k).start()
+            if role is None:
+                out[span(k * out_rows, out_rows), :] = val
+                return
+            send_buf[span(k * out_rows, out_rows), :] = val
+            if role == "lead":
+
+                @pl.when(step < 2)
+                def _():
+                    swap_copy(2 * k).start()
+                    swap_copy(2 * k + 1).start()
+
             else:
-                out[span(k * out_rows, out_rows), :] = val
-
-    def receive():
+                swap_copy(2 * k).start()
+
+                @pl.when(k == chunks - 1)
+                def _():
+                    swap_copy(2 * k + 1).start()
+
+                @pl.when(k < chunks - 1)
+                def _():
+                    relay_copy(k).start()
+
+    def pass_on():
+        for k in relayed:
+            relay_copy(k).wait_recv()
+            onward_copy(k).start()
+        for q in direct_late:
+            swap_copy(q).start()
+
+    def receive(role):
         swap_copy(0).wait_recv()
-        if chunks > 1:
-            swap_copy(chunks - 1).wait_recv()
+        swap_copy(2 * chunks - 1).wait_recv()
+        if piece < 2:
+            swap_copy(2 * chunks - 2).wait_recv()
         halo_send_up(2, r_buf, 2, r_buf)
         halo_send_down(2, r_buf, 2, r_buf)
-        for k in range(1, chunks - 1):
-            swap_copy(k).wait_recv()
+        skip = (0, 2 * chunks - 1) if piece >= 2 else (0, 2 * chunks - 1, 2 * chunks - 2)
+        for q in direct_back if role == "lead" else range(2 * chunks):
+            if q not in skip:
+                swap_copy(q).wait_recv()
+        if role == "lead":
+            for k in relayed:
+                onward_copy(k).wait_recv()
         halo_wait(2, r_buf, 2, r_buf)
 
     def weight_grad(j, lhs_t, src3, first):
@@ -321,29 +395,52 @@
 
         pair_copy(j).start()
 
+    def diag_copy(j):
+        return pltpu.make_async_remote_copy(
+            src_ref=tsend.at[j],
+            dst_ref=trecv.at[j],
+            send_sem=diag_s.at[j],
+            recv_sem=diag_r.at[j],
+            device_id=twin,
+            device_id_type=MESH,
+        )
+
+    def grads_to_diag(j):
+        pair_copy(j).wait_recv()
+
+        @pl.loop(0, nz)
+        def _(z):
+            other = gacc[j, parity, z, :, twin_lanes]
+            tsend[j, z] = (other + pair_in[j, z, :, twin_lanes].astype(F32)).astype(BF16)
+
+        diag_copy(j).start()
+
+    def summed(j, z):
+        own = gacc[j, parity, z, :, my_lanes] + pair_in[j, z, :, my_lanes].astype(F32)
+        return own + trecv[j, z].astype(F32)
+
     def grads_to_line(j):
-        pair_copy(j).wait_recv()
+        diag_copy(j).wait_recv()
 
         @pl.loop(0, nz - 1)
         def _(k):
-            z = lax.rem(mine + k + 1, nz)
-            zsend[j, k] = (gacc[j, parity, z] + pair_in[j, z].astype(F32)).astype(BF16)
+            zsend[j, k] = summed(j, lax.rem(mine + k + 1, nz)).astype(BF16)
             z_copy(j, k).start()
 
-        owned[j] = gacc[j, parity, mine] + pair_in[j, mine].astype(F32)
+        owned[j] = summed(j, mine)
 
     def grads_to_twin(j):
         total = owned[j]
         for k in range(nz - 1):
             z_copy(j, k).wait_recv()
             total = total + zrecv[j, k].astype(F32)
-        owned[j] = total
+        gout[j, :, my_lanes] = total
         psend[j] = total.astype(BF16)
         part_copy(j).start()
 
     def grads_finish(j):
         part_copy(j).wait_recv()
-        gout[j] = owned[j] + precv[j].astype(F32)
+        gout[j, :, twin_lanes] = precv[j].astype(F32)
 
     mid = slice(0, ch)
 
@@ -351,41 +448,55 @@
     def _():
         widen_all(a_buf, x3)
         hidden_forward(x3, y3)
-        finish_section(a_buf, y3, w3, 1, True)
+        finish_section(a_buf, y3, w3, 1, "lead")
         widen_all(s_buf, x3)
-        hidden_backward(x3, y3)
-        transposed(h_t, y3, 1, mid)
+        hidden_backward(x3, h_buf)
+        pass_on()
+        transpose_kernels()
+        transposed(h_t, h_buf, 1, mid)
         transposed(x_t, s_buf, 2, mid)
-        receive()
+        receive("lead")
         widen_all(r_buf, x3)
         weight_grad(1, h_t, x3, 1)
         grads_to_pair(1)
         inner_backward(x3, y3)
-        grads_to_line(1)
+        grads_to_diag(1)
         weight_grad(0, x_t, y3, 0)
         grads_to_pair(0)
-        finish_section(r_buf, y3, wt3, 0, False)
+        grads_to_line(1)
+        grads_to_diag(0)
+        finish_section(r_buf, y3, wt3, 0, None)
         grads_to_line(0)
+        for q in range(2 * chunks):
+            swap_copy(q).wait_send()
+        for k in relayed:
+            onward_copy(k).wait_send()
 
     @pl.when(jnp.logical_not(lead))
     def _():
         widen_all(s_buf, x3)
-        hidden_backward(x3, y3)
-        transposed(h_t, y3, 1, mid)
+        hidden_backward(x3, h_buf)
         widen_all(a_buf, x3)
         inner_backward(x3, y3)
-        finish_section(a_buf, y3, wt3, 0, True)
+        finish_section(a_buf, y3, wt3, 0, "lag")
+        transposed(h_t, h_buf, 1, mid)
         weight_grad(1, h_t, x3, 1)
         grads_to_pair(1)
         transposed(x_t, s_buf, 2, mid)
         weight_grad(0, x_t, y3, 0)
+        grads_to_pair(0)
+        for q in direct_back:
+            swap_copy(q).wait_send()
+        for k in relayed:
+            relay_copy(k).wait_send()
+        grads_to_diag(1)
+        grads_to_diag(0)
         grads_to_line(1)
-        grads_to_pair(0)
         grads_to_line(0)
-        receive()
+        receive("lag")
         widen_all(r_buf, x3)
         hidden_forward(x3, y3)
-        finish_section(r_buf, y3, w3, 1, False)
+        finish_section(r_buf, y3, w3, 1, None)
 
     grads_to_twin(1)
     grads_to_twin(0)
@@ -395,10 +506,9 @@
     halo_drain(0, arr, 0, a_buf)
     halo_drain(1, sta, 0, s_buf)
     halo_drain(2, r_buf, 2, r_buf)
-    for k in range(chunks):
-        swap_copy(k).wait_send()
     for j in range(2):
         pair_copy(j).wait_send()
+        diag_copy(j).wait_send()
         part_copy(j).wait_send()
         for k in range(nz - 1):
             z_copy(j, k).wait_send()
@@ -409,7 +519,10 @@
     n = lax.axis_size("space")
     nz, share = n // 2, ch // n
     scale = 1.0 / math.sqrt(rows * n * cols)
-    out_chunks = rows // divisor(rows, 4)
+    out_rows = divisor(rows, 4)
+    out_chunks = rows // out_rows
+    relays = max(out_chunks - 1, 1)
+    half = 9 * ch // 2
     cells = rows * cols
     wide = 9 * ch
     dma = pltpu.SemaphoreType.DMA
@@ -432,28 +545,38 @@
             vm((halo_cells, 3 * ch), BF16),
             vm((halo_cells, 3 * ch), BF16),
             vm(((rows + 2) * cols, ch), F32),
+            vm(((rows + 2) * cols, ch), BF16),
             vm((ch, cells), BF16),
             vm((ch, cells), BF16),
             vm((cells, ch), BF16),
             vm((2, 2, nz, share, wide), F32),
             vm((2, nz, share, wide), BF16),
             vm((2, nz, share, wide), BF16),
-            vm((2, nz - 1, share, wide), BF16),
-            vm((2, nz - 1, share, wide), BF16),
-            vm((2, share, wide), F32),
-            vm((2, share, wide), BF16),
-            vm((2, share, wide), BF16),
+            vm((2, nz - 1, share, half), BF16),
+            vm((2, nz - 1, share, half), BF16),
+            vm((2, share, half), F32),
+            vm((2, nz, share, half), BF16),
+            vm((2, nz, share, half), BF16),
+            vm((2, share, half), BF16),
+            vm((2, share, half), BF16),
+            vm((relays, out_rows // 2 * cols, ch), BF16),
             dma((3,)),
             dma((3, 2)),
             dma((3, 2)),
-            dma((out_chunks,)),
-            dma((out_chunks,)),
+            dma((2 * out_chunks,)),
+            dma((2 * out_chunks,)),
             dma((2,)),
             dma((2,)),
             dma((2, nz - 1)),
             dma((2, nz - 1)),
             dma((2,)),
             dma((2,)),
+            dma((2,)),
+            dma((2,)),
+            dma((relays,)),
+            dma((relays,)),
+            dma((relays,)),
+            dma((relays,)),
         ],
         compiler_params=pltpu.CompilerParams(
             collective_id=0, has_side_effects=True, vmem_limit_bytes=56 * 1024 * 1024

time: 85.4 us -> 80.1 us (0.938)
  Pallas kernels: 80.9 us -> 75 us
    pallas_call x1, Pallas kernels: 80.9 us -> 75 us  [body(): pl.pallas_call(functools.partial(kernel, (rows, cols, ch, n, scale)), out...]
where the time goes in v1:
time: 80.1 us; the launch traced here: 79.3 us
  Pallas kernels  75 us (94%)
  local copies, waits for them, and re-layouts  3.7 us (5%)
    pallas_call x1, Pallas kernels, body(): pl.pallas_call(functools.partial(kernel, (rows, cols, ch, n, scale)), out...  75 us
    unnamed x4, local copies, waits for them, and re-layouts  2.25 us

profile of v1, /device:TPU:24, one launch (start us, length us, event | category | flops | bytes accessed | tf_op | source)
XLA Modules:
  0.0 79.3 jit_solution(18176646585695064029)
XLA Ops:
  0.6 75.0 %shard_map.50 = (bf16[2048,256]{1,0:T(8,128)(2,1)}, f32[2,32,2304]{2,1,0:T(8,128)}) custom-call(bf16[2048,256]{1,0:T(8,128)(2,1)} %bitcast.9, bf16[2048,256]{1,0:T(8,128)(2,1)} %bitcast.10, bf16[2,3,768,256]{3,2,1,0:T(8,128)(2,1)} %bitcast.8), custom_call_target="tpu_custom_call" | custom-call | tf_op jit(solution)/shard_map/pallas_call | solution.py:531
  75.6 0.0 copy-start
  75.6 1.5 %reshape.23 = f32[2,32,3,3,256]{4,3,2,1,0:T(4,128)S(1)} reshape(f32[2,32,2304]{2,1,0:T(8,128)} %get-tuple-element.5) | data formatting | bytes 1179648 | tf_op jit(solution)/shard_map/reshape | solution.py:589
  77.1 1.3 %copy.6 = f32[1,1,32,2,3,3,256]{6,3,5,4,2,1,0:T(2,128)} copy(f32[1,1,32,2,3,3,256]{6,5,4,2,3,1,0:T(4,128)S(1)} %bitcast.7) | data formatting | bytes 1179648
  78.4 0.0 copy-done
  78.4 1.0 %copy.8 = bf16[1,1,16,128,256]{4,3,2,1,0:T(8,128)(2,1)} copy(bf16[1,1,16,128,256]{4,3,2,1,0:T(8,128)(2,1)S(1)} %bitcast.11) | data formatting | bytes 2097152
Async XLA Ops:
  75.6 2.7 %copy-start = (bf16[2048,256]{1,0:T(8,128)(2,1)S(1)}, bf16[2048,256]{1,0:T(8,128)(2,1)}, u32[]{:S(2)}) copy-start(bf16[2048,256]{1,0:T(8,128)(2,1)} %get-tuple-element.4) | copy-start | bytes 3145732
